TPU v7x, 32 devices: a whole 2x2x4 slice. The times are simulated.
32 devices in a mesh: src: 4 (over x, core), frame: 2 (over y), tile: 4 (over z).
Axes of the slice: x: 2, y: 2, z: 4, core: 2. Of those that a mesh axis runs over, the one named last changes fastest.
Arguments:
- feats: float32 [49152, 512], P(('src', 'frame', 'tile')), may hold values from -40 to 40
- row_map: int32 [49152], P(('src', 'frame', 'tile')), may hold values from 0 to 49151, as said below
- clip_ids: int32 [12], replicated, may hold values from 0 to 3, never falling along the last dimension, each value on 1 to 6 neighbouring positions
- norm_gain: float32 [512], replicated, may hold values from 0.1 to 1.9
- norm_bias: float32 [512], replicated, may hold values from -3 to 3
- conv_weight: bfloat16 [3, 3, 3, 512, 512], replicated, may hold values from -0.0546875 to 0.0546875
- conv_bias: float32 [512], replicated, may hold values from -2 to 2
Outputs:
- decoded: bfloat16 [12, 32, 128, 512], P('frame', 'tile', 'src')
Inputs may be any that keep to these rules, and one draw needn't show every extreme that they name: `row_map`: every decoder index occurs once; the rows of each device of src+frame+tile hold exactly 48 indices of each aligned block of 1536 decoder indices. `clip_ids`: clip numbers never fall along the frames; each clip has 1 to 6 frames, one exactly 6.
All inputs are finite; a program needn't handle non-finite values.
Results may differ from a plain program's by a relative error of at most 0.0029.
Values may be sent and summed in bfloat16 or wider, within the bound.
A program may use at most 128 MiB of HBM per device.

v0:
```python
import jax
import jax.numpy as jnp
from jax import lax
from jax.sharding import PartitionSpec as P

GROUPS = 32
CLIPS = 4
FR_DEV = 6
HR = 8
WCOL = 32


def passed_along(x, axis, by):
    peers = lax.axis_size(axis)
    pairs = [(i, i + by) for i in range(peers) if 0 <= i + by < peers]
    return lax.ppermute(x, axis, pairs)


def with_halo(x, sides, width):
    for axis, dim in sides:
        peers, length = (lax.axis_size(axis), x.shape[dim])
        up = [(i, (i + 1) % peers) for i in range(peers - 1)]
        down = [(j, i) for i, j in up]
        last = lax.slice_in_dim(x, length - width, length, axis=dim)
        leading = lax.slice_in_dim(x, 0, width, axis=dim)
        before = lax.ppermute(last, axis, up)
        after = lax.ppermute(leading, axis, down)
        x = jnp.concatenate([before, x, after], axis=dim)
    return x


def shards(feats, row_map, clip_ids, norm_gain, norm_bias, conv_weight, conv_bias):
    local_rows, channels = feats.shape
    n_src = lax.axis_size("src")
    n_frame = lax.axis_size("frame")
    n_tile = lax.axis_size("tile")
    devices = n_src * n_frame * n_tile
    per_pair = local_rows // devices
    owners = row_map // local_rows
    ordering = jnp.argsort(owners, stable=True)
    outgoing = feats[ordering]
    slot_ids = (row_map % local_rows)[ordering]
    arrived, targets = (
        lax.all_to_all(
            outgoing.reshape(devices, per_pair, channels),
            ("src", "frame", "tile"),
            split_axis=0,
            concat_axis=0,
            tiled=True,
        ),
        lax.all_to_all(
            slot_ids.reshape(devices, per_pair),
            ("src", "frame", "tile"),
            split_axis=0,
            concat_axis=0,
            tiled=True,
        ),
    )
    inverse = jnp.argsort(targets.reshape(-1))
    features = arrived.reshape(-1, channels)[inverse].reshape(FR_DEV, HR, WCOL, channels)
    first_frame = lax.axis_index("frame") * FR_DEV
    padded_ids = jnp.concatenate([jnp.full((2,), -1, jnp.int32), clip_ids])
    window_ids = lax.dynamic_slice_in_dim(padded_ids, first_frame, FR_DEV + 2)
    own_ids = window_ids[2:]
    onehot = (own_ids[:, None] == jnp.arange(CLIPS, dtype=jnp.int32)[None, :]).astype(jnp.float32)
    group_width = channels // GROUPS
    all_onehot = (clip_ids[:, None] == jnp.arange(CLIPS, dtype=jnp.int32)[None, :]).astype(
        jnp.float32
    )
    counts = jnp.sum(all_onehot, axis=0) * (HR * n_tile * WCOL * n_src * group_width)
    shaped = features.reshape(FR_DEV, HR * WCOL, GROUPS, group_width)
    frame_sum = jnp.sum(shaped, axis=(1, 3))
    local_sum = jnp.dot(onehot.T, frame_sum, precision=lax.Precision.HIGHEST)
    clip_mean = lax.psum(local_sum, ("src", "frame", "tile")) / counts[:, None]
    frame_mean = jnp.dot(onehot, clip_mean, precision=lax.Precision.HIGHEST)
    centred = shaped - frame_mean[:, None, :, None]
    frame_sq = jnp.sum(centred * centred, axis=(1, 3))
    local_sq = jnp.dot(onehot.T, frame_sq, precision=lax.Precision.HIGHEST)
    clip_var = lax.psum(local_sq, ("src", "frame", "tile")) / counts[:, None]
    inverse_std = 1.0 / jnp.sqrt(clip_var + 1e-06)
    frame_inv = jnp.dot(onehot, inverse_std, precision=lax.Precision.HIGHEST)
    normed = (centred * frame_inv[:, None, :, None]).reshape(FR_DEV, HR, WCOL, channels)
    activated = jax.nn.silu(normed * norm_gain + norm_bias).astype(jnp.bfloat16)
    previous = passed_along(activated[FR_DEV - 2 :], "frame", 1)
    extended = jnp.concatenate([previous, activated], axis=0)
    padded = with_halo(extended, (("tile", 1), ("src", 2)), 1)
    conv_sum = jnp.zeros((FR_DEV, HR * WCOL, channels), jnp.float32)
    for tap_time in range(3):
        validity = (window_ids[tap_time : tap_time + FR_DEV] == own_ids).astype(jnp.float32)
        partial_value = jnp.zeros((FR_DEV * HR * WCOL, channels), jnp.float32)
        for tap_high in range(3):
            stacked = jnp.concatenate(
                [
                    padded[
                        tap_time : tap_time + FR_DEV,
                        tap_high : tap_high + HR,
                        tap_wide : tap_wide + WCOL,
                        :,
                    ]
                    for tap_wide in range(3)
                ],
                axis=-1,
            )
            kernel = conv_weight[tap_time, tap_high].reshape(3 * channels, channels)
            partial_value = partial_value + jnp.dot(
                stacked.reshape(-1, 3 * channels), kernel, preferred_element_type=jnp.float32
            )
        conv_sum = (
            conv_sum + partial_value.reshape(FR_DEV, HR * WCOL, channels) * validity[:, None, None]
        )
    decoded = features + conv_sum.reshape(FR_DEV, HR, WCOL, channels) + conv_bias
    return decoded.astype(jnp.bfloat16)


def solution(mesh):
    placed = (
        P(("src", "frame", "tile"), None),
        P(("src", "frame", "tile")),
        P(),
        P(),
        P(),
        P(),
        P(),
    )
    return jax.shard_map(
        shards,
        mesh=mesh,
        in_specs=placed,
        out_specs=P("frame", "tile", "src", None),
        check_vma=False,
    )
```

profile of v0, /device:TPU:1, one launch (start us, length us, event | category | flops | bytes accessed | tf_op | source)
XLA Modules:
  0.0 304.1 jit_solution(15741347059751601418)
XLA Ops:
  0.0 0.9 add_select_fusion
  0.9 5.0 %sort.34 = (s32[1536]{0:T(1024)}, s32[1536]{0:T(1024)S(1)}) sort(s32[1536]{0:T(1024)S(1)} %get-tuple-element.53, s32[1536]{0:T(1024)S(1)} %iota.14), dimensions={0}, to_apply=%region_0.1 | sort | flops 16896 | bytes 24576 | tf_op jit(solution)/shard_map/jit(argsort)/sort | solution.py:40
  5.9 8.4 %gather_fusion.1 = s32[1536]{0:T(1024)S(1)} fusion(s32[1536]{0:T(1024)S(1)} %get-tuple-element.52, s32[2048]{0:T(1024)S(1)} %pad_clamp_fusion.1), kind=kCustom, calls=%fused_computation.1 | custom fusion | bytes 18432 | tf_op jit(solution)/shard_map/gather | solution.py:42
  15.0 7.1 %all-to-all-start.1 = ((s32[32,1,48]{2,1,0:T(1,128)}), s32[32,1,48]{2,1,0:T(1,128)S(1)}, u32[]{:S(2)}, u32[]{:S(2)}) async-start(s32[32,1,48]{2,1,0:T(1,128)} %all_to_all.10), calls=%async_computation.1 | async-start | bytes 32768 | tf_op jit(solution)/shard_map/all_to_all | solution.py:51
  22.1 5.0 %gather_fusion = f32[1536,512]{1,0:T(8,128)} fusion(f32[1536,512]{1,0:T(8,128)S(1)} %copy-done, s32[2048]{0:T(1024)S(1)} %pad_clamp_fusion.1), kind=kCustom, calls=%fused_computation | custom fusion | bytes 6297600 | tf_op jit(solution)/shard_map/gather | solution.py:41
  27.1 1.7 all-to-all-done.1
  28.7 4.2 %all-to-all-start = ((f32[32,48,512]{2,1,0:T(8,128)}), f32[32,48,512]{2,1,0:T(8,128)S(1)}, u32[]{:S(2)}, u32[]{:S(2)}) async-start(f32[32,48,512]{2,1,0:T(8,128)} %bitcast.49), calls=%async_computation | async-start | bytes 6291456 | tf_op jit(solution)/shard_map/all_to_all | solution.py:44
  34.5 5.0 %sort.35 = (s32[1536]{0:T(1024)}, s32[1536]{0:T(1024)S(1)}) sort(s32[1536]{0:T(1024)S(1)} %reshape.75, s32[1536]{0:T(1024)S(1)} %iota.15), dimensions={0}, to_apply=%region_1.2 | sort | flops 16896 | bytes 24576 | tf_op jit(solution)/shard_map/jit(argsort)/sort | solution.py:59
  39.6 62.9 %all-to-all-done = f32[32,48,512]{2,1,0:T(8,128)S(1)} async-done(((f32[32,48,512]{2,1,0:T(8,128)}), f32[32,48,512]{2,1,0:T(8,128)S(1)}, u32[]{:S(2)}, u32[]{:S(2)}) %all-to-all-start) | async-done | bytes 3145760 | tf_op jit(solution)/shard_map/all_to_all | solution.py:44
  102.5 4.9 %gather_fusion.2 = f32[1536,512]{1,0:T(8,128)} fusion(f32[1536,512]{1,0:T(8,128)S(1)} %bitcast.46, s32[2048]{0:T(1024)S(1)} %pad_clamp_fusion), kind=kCustom, calls=%fused_computation.2 | custom fusion | bytes 6297600 | tf_op jit(solution)/shard_map/gather | solution.py:60
  107.4 2.4 copy.12
  109.8 2.5 reshape_reshape.3
  112.3 2.6 reduce_sum.27
  115.1 40.2 %psum.14 = f32[4,32]{1,0:T(4,128)S(1)} all-reduce(f32[4,32]{1,0:T(4,128)S(1)} %fusion.9), channel_id=1, replica_groups=mesh['src'=4,'frame'=2,'tile'=4] {'src','frame','tile'}, use_global_device_ids=true, to_apply=%region_3.4 | all-reduce | flops 128 | bytes 1024 | tf_op jit(solution)/shard_map/psum | solution.py:74
  155.5 2.9 multiply_reduce_fusion
  158.7 38.8 %psum.15 = f32[4,32]{1,0:T(4,128)S(1)} all-reduce(f32[4,32]{1,0:T(4,128)S(1)} %fusion.7), channel_id=1, replica_groups=mesh['src'=4,'frame'=2,'tile'=4] {'src','frame','tile'}, use_global_device_ids=true, to_apply=%region_6.7 | all-reduce | flops 128 | bytes 1024 | tf_op jit(solution)/shard_map/psum | solution.py:79
  198.1 2.9 multiply_convert_fusion
  201.0 3.6 %collective-permute-start = (bf16[2,8,32,512]{3,2,1,0:T(8,128)(2,1)S(1)}, bf16[2,8,32,512]{3,2,1,0:T(8,128)(2,1)S(1)}, u32[]{:S(2)}, u32[]{:S(2)}) collective-permute-start(bf16[2,8,32,512]{3,2,1,0:T(8,128)(2,1)S(1)} %slice.203), channel_id=1, source_target_pairs={{0,4},{1,5},{2,6},{3,7},{8,12},{9,13},{10,14},{11,15},{16,20},{17,... | collective-permute-start | bytes 1572872 | tf_op jit(solution)/shard_map/ppermute | solution.py:16
  204.6 9.6 %fusion.23 = (bf16[1,1,3,512,512]{4,3,2,1,0:T(8,128)(2,1)}, bf16[1,1,3,512,512]{4,3,2,1,0:T(8,128)(2,1)}, bf16[1,1,3,512,512]{4,3,2,1,0:T(8,128)(2,1)}, bf16[1,1...) fusion(bf16[3,3,3,512,512]{4,3,2,1,0:T(8,128)(2,1)} %param.12), kind=kLoop, calls=%fused_computation.69 | loop fusion | bytes 28311552 | tf_op jit(solution)/shard_map/slice | solution.py:104
  214.2 3.9 %collective-permute-start.1 = (bf16[8,1,32,512]{3,2,1,0:T(8,128)(2,1)S(1)}, bf16[8,1,32,512]{3,2,1,0:T(8,128)(2,1)S(1)}, u32[]{:S(2)}, u32[]{:S(2)}) collective-permute-start(bf16[8,1,32,512]{3,2,1,0:T(8,128)(2,1)S(1)} %get-tuple-element.48), channel_id=1, source_target_pairs={{0,1},{1,2},{2,3},{4,5},{5,6},{6,7},{8,9},{9,10},{10,11},{12,13},{... | collective-permute-start | bytes 786440 | tf_op jit(solution)/shard_map/ppermute | solution.py:26
  218.2 1.3 collective-permute-start.2
  219.7 1.8 collective-permute-done.1
  221.4 3.8 %collective-permute-done.2 = bf16[8,1,32,512]{3,2,1,0:T(8,128)(2,1)S(1)} collective-permute-done((bf16[8,1,32,512]{3,2,1,0:T(8,128)(2,1)S(1)}, bf16[8,1,32,512]{3,2,1,0:T(8,128)(2,1)S(1)}, u32[]{:S(2)}, u32[]{:S(2)}) %collective-permute-start.2) | collective-permute-done | bytes 262176 | tf_op jit(solution)/shard_map/ppermute | solution.py:27
  225.5 6.1 %collective-permute-start.3 = (bf16[8,10,1,512]{3,2,1,0:T(2,128)(2,1)S(1)}, bf16[8,10,1,512]{3,2,1,0:T(2,128)(2,1)S(1)}, u32[]{:S(2)}, u32[]{:S(2)}) collective-permute-start(bf16[8,10,1,512]{3,2,1,0:T(2,128)(2,1)S(1)} %get-tuple-element.38), channel_id=1, source_target_pairs={{0,8},{8,16},{16,24},{1,9},{9,17},{17,25},{2,10},{10,18},{18,26},{... | collective-permute-start | bytes 245768 | tf_op jit(solution)/shard_map/ppermute | solution.py:26
  231.6 2.1 collective-permute-start.4
  234.3 1.5 fusion.26
  235.8 2.4 collective-permute-done.4
  238.2 2.4 maximum_maximum_fusion
  240.6 4.3 %fusion.24 = (bf16[6,8,32,512]{3,2,1,0:T(8,128)(2,1)}, bf16[6,8,32,512]{3,2,1,0:T(8,128)(2,1)S(1)}, bf16[6,8,32,512]{3,2,1,0:T(8,128)(2,1)}, bf16[6,8,32,512]{3,...) fusion(bf16[8,10,33,512]{3,2,1,0:T(8,128)(2,1)S(1)} %get-tuple-, ...), kind=kLoop, calls=%fused_computation.70 | loop fusion | bytes 28311552 | tf_op jit(solution)/shard_map/slice | solution.py:94
  244.9 10.4 %fusion.25 = (bf16[6,8,32,512]{3,2,1,0:T(8,128)(2,1)}, bf16[6,8,32,512]{3,2,1,0:T(8,128)(2,1)}, bf16[6,8,32,512]{3,2,1,0:T(8,128)(2,1)}, bf16[6,8,32,512]{3,2,1,...) fusion(bf16[8,10,33,512]{3,2,1,0:T(8,128)(2,1)S(1)} %get-tuple-, ...), kind=kLoop, calls=%fused_computation.71 | loop fusion | bytes 28311552 | tf_op jit(solution)/shard_map/slice | solution.py:94
  255.3 2.3 pad_maximum_fusion.2
  257.7 4.3 %fusion.28 = f32[1536,512]{1,0:T(8,128)} fusion(bf16[1536,1536]{1,0:T(8,128)(2,1)S(1)} %bitcast.56, bf16[1536,512]{1,0:T(8,128)(2,1)S(1)} %bitcast.70), kind=kOutput, calls=%fused_computation.74 | convolution fusion | flops 2415919104 | bytes 9437184 | tf_op jit(solution)/shard_map/dot_general | solution.py:105
  262.0 1.0 fusion.1
  262.9 5.8 %fusion.29 = f32[1536,512]{1,0:T(8,128)} fusion(bf16[1536,1536]{1,0:T(8,128)(2,1)S(1)} %bitcast.58, bf16[1536,512]{1,0:T(8,128)(2,1)} %bitcast.69), kind=kOutput, calls=%fused_computation.75 | convolution fusion | flops 2415919104 | bytes 9437184 | tf_op jit(solution)/shard_map/dot_general | solution.py:105
  268.7 4.3 %fusion.30 = f32[1536,512]{1,0:T(8,128)} fusion(bf16[1536,1536]{1,0:T(8,128)(2,1)S(1)} %bitcast.57, bf16[1536,512]{1,0:T(8,128)(2,1)S(1)} %bitcast.68), kind=kOutput, calls=%fused_computation.76 | convolution fusion | flops 2415919104 | bytes 9437184 | tf_op jit(solution)/shard_map/dot_general | solution.py:105
  273.5 0.9 copy-done.7
  276.3 1.0 copy-done.30
  277.2 2.7 convolution_add_fusion.5
  280.0 2.8 convolution_add_fusion.4
  283.3 0.9 copy-done.3
  285.1 1.0 copy-done.19
  286.1 1.0 copy-done.29
  287.1 2.8 convolution_add_fusion.3
  290.0 2.8 convolution_add_fusion.2
  294.6 1.0 copy-done.28
  295.6 2.7 convolution_add_fusion.1
  298.4 2.8 convolution_add_fusion
  301.2 2.9 add_convert_fusion
  (93 shorter events, 10.4 us)
Async XLA Ops:
  0.0 22.1 %copy-start = (f32[1536,512]{1,0:T(8,128)S(1)}, f32[1536,512]{1,0:T(8,128)}, u32[]{:S(2)}) copy-start(f32[1536,512]{1,0:T(8,128)} %param.7) | copy-start | bytes 9437188
  15.0 13.7 %all-to-all-start.1 = ((s32[32,1,48]{2,1,0:T(1,128)}), s32[32,1,48]{2,1,0:T(1,128)S(1)}, u32[]{:S(2)}, u32[]{:S(2)}) async-start(s32[32,1,48]{2,1,0:T(1,128)} %all_to_all.10), calls=%async_computation.1 | async-start | bytes 32768 | tf_op jit(solution)/shard_map/all_to_all | solution.py:51
  28.7 4.2 %copy-start.27 = (s32[12]{0:T(128)S(1)}, s32[12]{0:T(128)}, u32[]{:S(2)}) copy-start(s32[12]{0:T(128)} %param.9) | copy-start | bytes 148
  28.7 73.7 %all-to-all-start = ((f32[32,48,512]{2,1,0:T(8,128)}), f32[32,48,512]{2,1,0:T(8,128)S(1)}, u32[]{:S(2)}, u32[]{:S(2)}) async-start(f32[32,48,512]{2,1,0:T(8,128)} %bitcast.49), calls=%async_computation | async-start | bytes 6291456 | tf_op jit(solution)/shard_map/all_to_all | solution.py:44
  114.8 83.2 %copy-start.24 = (f32[512]{0:T(512)S(1)}, f32[512]{0:T(512)}, u32[]{:S(2)}) copy-start(f32[512]{0:T(512)} %param.11) | copy-start | bytes 6148
  114.8 83.3 %copy-start.25 = (f32[512]{0:T(512)S(1)}, f32[512]{0:T(512)}, u32[]{:S(2)}) copy-start(f32[512]{0:T(512)} %param.10) | copy-start | bytes 6148
  201.0 13.2 %collective-permute-start = (bf16[2,8,32,512]{3,2,1,0:T(8,128)(2,1)S(1)}, bf16[2,8,32,512]{3,2,1,0:T(8,128)(2,1)S(1)}, u32[]{:S(2)}, u32[]{:S(2)}) collective-permute-start(bf16[2,8,32,512]{3,2,1,0:T(8,128)(2,1)S(1)} %slice.203), channel_id=1, source_target_pairs={{0,4},{1,5},{2,6},{3,7},{8,12},{9,13},{10,14},{11,15},{16,20},{17,... | collective-permute-start | bytes 1572872 | tf_op jit(solution)/shard_map/ppermute | solution.py:16
  214.2 7.2 %collective-permute-start.1 = (bf16[8,1,32,512]{3,2,1,0:T(8,128)(2,1)S(1)}, bf16[8,1,32,512]{3,2,1,0:T(8,128)(2,1)S(1)}, u32[]{:S(2)}, u32[]{:S(2)}) collective-permute-start(bf16[8,1,32,512]{3,2,1,0:T(8,128)(2,1)S(1)} %get-tuple-element.48), channel_id=1, source_target_pairs={{0,1},{1,2},{2,3},{4,5},{5,6},{6,7},{8,9},{9,10},{10,11},{12,13},{... | collective-permute-start | bytes 786440 | tf_op jit(solution)/shard_map/ppermute | solution.py:26
  218.2 7.1 %collective-permute-start.2 = (bf16[8,1,32,512]{3,2,1,0:T(8,128)(2,1)S(1)}, bf16[8,1,32,512]{3,2,1,0:T(8,128)(2,1)S(1)}, u32[]{:S(2)}, u32[]{:S(2)}) collective-permute-start(bf16[8,1,32,512]{3,2,1,0:T(8,128)(2,1)S(1)} %get-tuple-element.49), channel_id=1, source_target_pairs={{1,0},{2,1},{3,2},{5,4},{6,5},{7,6},{9,8},{10,9},{11,10},{13,12},{... | collective-permute-start | bytes 786440 | tf_op jit(solution)/shard_map/ppermute | solution.py:27
  225.5 10.3 %collective-permute-start.3 = (bf16[8,10,1,512]{3,2,1,0:T(2,128)(2,1)S(1)}, bf16[8,10,1,512]{3,2,1,0:T(2,128)(2,1)S(1)}, u32[]{:S(2)}, u32[]{:S(2)}) collective-permute-start(bf16[8,10,1,512]{3,2,1,0:T(2,128)(2,1)S(1)} %get-tuple-element.38), channel_id=1, source_target_pairs={{0,8},{8,16},{16,24},{1,9},{9,17},{17,25},{2,10},{10,18},{18,26},{... | collective-permute-start | bytes 245768 | tf_op jit(solution)/shard_map/ppermute | solution.py:26
  231.6 6.6 %collective-permute-start.4 = (bf16[8,10,1,512]{3,2,1,0:T(2,128)(2,1)S(1)}, bf16[8,10,1,512]{3,2,1,0:T(2,128)(2,1)S(1)}, u32[]{:S(2)}, u32[]{:S(2)}) collective-permute-start(bf16[8,10,1,512]{3,2,1,0:T(2,128)(2,1)S(1)} %get-tuple-element.39), channel_id=1, source_target_pairs={{8,0},{16,8},{24,16},{9,1},{17,9},{25,17},{10,2},{18,10},{26,18},{... | collective-permute-start | bytes 245768 | tf_op jit(solution)/shard_map/ppermute | solution.py:27
  255.3 2.4 copy-start.23
  257.7 4.3 %copy-start.11 = (bf16[6,8,32,512]{3,2,1,0:T(8,128)(2,1)S(1)}, bf16[6,8,32,512]{3,2,1,0:T(8,128)(2,1)}, u32[]{:S(2)}) copy-start(bf16[6,8,32,512]{3,2,1,0:T(8,128)(2,1)} %get-tuple-element.20) | copy-start | bytes 4718596
  257.7 4.3 %copy-start.12 = (bf16[6,8,32,512]{3,2,1,0:T(8,128)(2,1)S(1)}, bf16[6,8,32,512]{3,2,1,0:T(8,128)(2,1)}, u32[]{:S(2)}) copy-start(bf16[6,8,32,512]{3,2,1,0:T(8,128)(2,1)} %get-tuple-element.23) | copy-start | bytes 4718596
  257.7 4.3 %copy-start.14 = (bf16[6,8,32,512]{3,2,1,0:T(8,128)(2,1)S(1)}, bf16[6,8,32,512]{3,2,1,0:T(8,128)(2,1)}, u32[]{:S(2)}) copy-start(bf16[6,8,32,512]{3,2,1,0:T(8,128)(2,1)} %get-tuple-element.29) | copy-start | bytes 4718596
  257.7 4.3 %copy-start.15 = (bf16[6,8,32,512]{3,2,1,0:T(8,128)(2,1)S(1)}, bf16[6,8,32,512]{3,2,1,0:T(8,128)(2,1)}, u32[]{:S(2)}) copy-start(bf16[6,8,32,512]{3,2,1,0:T(8,128)(2,1)} %get-tuple-element.32) | copy-start | bytes 4718596
  262.9 5.8 %copy-start.22 = (bf16[1,1,3,512,512]{4,3,2,1,0:T(8,128)(2,1)S(1)}, bf16[1,1,3,512,512]{4,3,2,1,0:T(8,128)(2,1)}, u32[]{:S(2)}) copy-start(bf16[1,1,3,512,512]{4,3,2,1,0:T(8,128)(2,1)} %get-tuple-element.17) | copy-start | bytes 4718596
  268.7 4.3 %copy-start.9 = (bf16[6,8,32,512]{3,2,1,0:T(8,128)(2,1)S(1)}, bf16[6,8,32,512]{3,2,1,0:T(8,128)(2,1)}, u32[]{:S(2)}) copy-start(bf16[6,8,32,512]{3,2,1,0:T(8,128)(2,1)} %get-tuple-element.18) | copy-start | bytes 4718596
  268.7 4.3 %copy-start.13 = (bf16[6,8,32,512]{3,2,1,0:T(8,128)(2,1)S(1)}, bf16[6,8,32,512]{3,2,1,0:T(8,128)(2,1)}, u32[]{:S(2)}) copy-start(bf16[6,8,32,512]{3,2,1,0:T(8,128)(2,1)} %get-tuple-element.27) | copy-start | bytes 4718596
  273.0 1.4 copy-start.7
  273.0 1.9 copy-start.10
  274.9 1.4 copy-start.21
  274.9 2.4 copy-start.30
  277.2 2.7 copy-start.20
  280.0 2.8 copy-start.5
  280.0 2.8 copy-start.8
  282.8 1.4 copy-start.3
  282.8 1.9 copy-start.6
  284.7 1.4 copy-start.19
  284.7 2.4 copy-start.29
  287.1 2.9 copy-start.18
  289.9 2.9 copy-start.4
  293.2 1.4 copy-start.17
  293.2 2.4 copy-start.28
  295.6 2.8 copy-start.16
  298.3 2.8 copy-start.2
  298.3 2.8 copy-start.26
  301.2 2.9 copy-start.1
where the time goes:
time: 305 us; the launch traced here: 304 us
  blocking collectives  79 us (26%)
  waiting for transfers between devices  72.6 us (24%)
  local copies, waits for them, and re-layouts  59.2 us (19%)
  other arithmetic  32.7 us (11%)
  matrix products  31.9 us (10%)
  starting transfers between devices  28.2 us (9%)
    all_to_all x1, waiting for transfers between devices, shards(): lax.all_to_all(outgoing.reshape(devices, per_pair, channels), ('src', 'fr...  62.9 us
    psum x1, blocking collectives, shards(): clip_mean = lax.psum(local_sum, ('src', 'frame', 'tile')) / counts[:, None]  40.2 us
    psum x1, blocking collectives, shards(): clip_var = lax.psum(local_sq, ('src', 'frame', 'tile')) / counts[:, None]  38.8 us
    dot_general x9, matrix products, shards(): jnp.dot(stacked.reshape(-1, 3 * channels), kernel, preferred_element_type...  31 us
    slice x3, local copies, waits for them, and re-layouts, shards(): padded[tap_time:tap_time + FR_DEV, tap_high:tap_high + HR, tap_wide:tap_w...  16.2 us
    ppermute x2, starting transfers between devices, with_halo(): before = lax.ppermute(last, axis, up)  9.97 us
    slice x1, local copies, waits for them, and re-layouts, shards(): kernel = conv_weight[tap_time, tap_high].reshape(3 * channels, channels)  9.59 us
    gather x1, local copies, waits for them, and re-layouts, shards(): slot_ids = (row_map % local_rows)[ordering]  8.39 us
  transfers between devices with their start and end apart: 7, of which 5 were waited for; matrix products, arithmetic and copies ran while one was open for 8% of the time, Pallas kernels for 0%

commit v1 on v0

v1 whole, which is shorter than its diff:
```python
import functools

import jax
import jax.numpy as jnp
from jax import lax
from jax.experimental import pallas as pl
from jax.experimental.pallas import tpu as pltpu
from jax.sharding import PartitionSpec as P

GROUPS = 32
CLIPS = 4
FR_DEV = 6
HR = 8
WCOL = 32
MESH = pl.DeviceIdType.MESH
BF = jnp.bfloat16
CODE = jnp.int16
STEPS = 1024.0
LOWEST = 26.6


F32 = jnp.float32
VMEM_LIMIT = 56 * 1024 * 1024


def dot(a, b):
    return jnp.dot(a, b, preferred_element_type=F32)


def dot_exact(a, b):
    return jnp.dot(a, b, preferred_element_type=F32, precision=lax.Precision.HIGHEST)


def iota(shape, dim):
    return lax.broadcasted_iota(jnp.int32, shape, dim)


def encode(x):
    octave = jnp.log2(jnp.maximum(jnp.abs(x), 1e-30)) + LOWEST
    code = jnp.clip(octave * STEPS + 0.5, 0.0, 32767.0).astype(jnp.int32)
    return jnp.where(x < 0.0, -code, code).astype(CODE)


def decode(code):
    code = code.astype(jnp.int32).astype(F32)
    size = jnp.abs(code)
    value = jnp.exp2(size * (1.0 / STEPS) - LOWEST)
    value = jnp.where(size < 1.0, 0.0, value)
    return jnp.where(code < 0.0, -value, value)


def split3(x):
    hi = x.astype(BF)
    rest = x - hi.astype(F32)
    mid = rest.astype(BF)
    low = (rest - mid.astype(F32)).astype(BF)
    return hi, mid, low


def group_matrix(channels, width):
    return (iota((channels, 128), 0) // width == iota((channels, 128), 1) % GROUPS).astype(F32)


def group_matrix_t(channels, width):
    return (iota((128, channels), 1) // width == iota((128, channels), 0) % GROUPS).astype(F32)


def clip_lanes():
    return iota((8, 128), 1) // GROUPS == iota((8, 128), 0)


def reshard_kernel(sizes, block, info_ref, feats_ref, arrived_ref, msgs_ref, packed, msg,
                   send_sem, recv_sem, msend_sem, mrecv_sem):
    n_src, n_frame, n_tile = sizes
    devices = n_src * n_frame * n_tile
    rows, channels = feats_ref.shape
    width = channels // GROUPS
    me = (lax.axis_index("src") * n_frame + lax.axis_index("frame")) * n_tile + lax.axis_index("tile")

    def coords(k):
        peer = lax.rem(me + k, devices)
        return (peer // (n_frame * n_tile), lax.rem(peer // n_tile, n_frame), lax.rem(peer, n_tile))

    barrier = pltpu.get_barrier_semaphore()

    def greet(k, carry):
        pl.semaphore_signal(barrier, inc=1, device_id=coords(k), device_id_type=MESH)
        return carry

    lax.fori_loop(1, devices, greet, 0)

    owner = info_ref[0:1, :]
    slot_hi = info_ref[1:2, :].astype(F32)
    slot_lo = info_ref[2:3, :].astype(F32)
    clip = info_ref[3:4, :]

    owner_is = iota((devices, rows), 0) == owner
    onehot = owner_is.astype(F32)
    onehot_b = onehot.astype(BF)
    span = 256
    before = (iota((span, span), 0) < iota((span, span), 1)).astype(F32).astype(BF)
    running = jnp.zeros((devices, 1), F32)
    ranks = []
    for start in range(0, rows, span):
        part = onehot[:, start : start + span]
        ahead = dot(onehot_b[:, start : start + span], before) + running
        ranks.append(jnp.sum(part * ahead, axis=0, keepdims=True))
        running = running + jnp.sum(part, axis=1, keepdims=True)
    rank = jnp.concatenate(ranks, axis=1).astype(jnp.int32)
    position = owner * block + rank
    hi, mid, low = split3(feats_ref[...])
    total = devices * block
    chunk = total // 4
    for start in range(0, total, chunk):
        pick = (iota((chunk, rows), 0) + start == position).astype(F32).astype(BF)
        packed[pl.ds(start, chunk), :] = encode(dot(pick, hi) + dot(pick, mid))

    pl.semaphore_wait(barrier, devices - 1)

    def row_copy(k):
        return pltpu.make_async_remote_copy(
            src_ref=packed.at[pl.ds(pl.multiple_of(k * block, 16), block)],
            dst_ref=arrived_ref.at[pl.ds(pl.multiple_of(me * block, 16), block)],
            send_sem=send_sem.at[k],
            recv_sem=recv_sem.at[k],
            device_id=coords(k),
            device_id_type=MESH,
        )

    def send_rows(k, carry):
        row_copy(k).start()
        return carry

    lax.fori_loop(1, devices, send_rows, 0)
    arrived_ref[pl.ds(pl.multiple_of(me * block, 16), block), :] = packed[0:block, :]

    rank_is = (iota((128, rows), 0) == rank).astype(F32).astype(BF)
    contract = (((1,), (1,)), ((), ()))
    ids = 32.0 * lax.dot_general(
        (onehot * slot_hi).astype(BF), rank_is, contract, preferred_element_type=F32
    ) + lax.dot_general((onehot * slot_lo).astype(BF), rank_is, contract, preferred_element_type=F32)

    in_clip = (iota((8, rows), 0) == clip).astype(F32)
    in_clip_b = in_clip.astype(BF)
    counts = jnp.sum(in_clip, axis=1, keepdims=True) * float(width)
    sums = dot(in_clip_b, hi) + dot(in_clip_b, mid) + dot(in_clip_b, low)
    to_groups = group_matrix(channels, width)
    group_sums = dot_exact(sums, to_groups)
    own_lanes = clip_lanes()
    means = jnp.where(iota((8, 128), 1) < GROUPS, group_sums / jnp.maximum(counts, 1.0), 0.0)
    m_hi, m_mid, m_low = split3(dot_exact(means, group_matrix_t(channels, width)))
    by_row = in_clip.T.astype(BF)
    centre = dot(by_row, m_hi) + dot(by_row, m_mid) + dot(by_row, m_low)
    centred = feats_ref[...] - centre
    s_hi, s_mid, s_low = split3(centred * centred)
    squares = dot(in_clip_b, s_hi) + dot(in_clip_b, s_mid) + dot(in_clip_b, s_low)
    group_squares = dot_exact(squares, to_groups)

    def lanes(x):
        return jnp.sum(jnp.where(own_lanes, x, 0.0), axis=0, keepdims=True)

    line = iota((8, 128), 0)
    stats = jnp.where(
        line == 1,
        lanes(group_sums),
        jnp.where(line == 2, lanes(group_squares),
                  jnp.where(line == 3, lanes(jnp.broadcast_to(counts, (8, 128))), 0.0)),
    )
    wide = (devices, 8, 128)
    msg[...] = jnp.where(
        iota(wide, 1) == 0,
        jnp.broadcast_to(ids[:, None, :], wide),
        jnp.broadcast_to(stats[None], wide),
    )

    def msg_copy(k):
        return pltpu.make_async_remote_copy(
            src_ref=msg.at[k],
            dst_ref=msgs_ref.at[me],
            send_sem=msend_sem.at[k],
            recv_sem=mrecv_sem.at[k],
            device_id=coords(k),
            device_id_type=MESH,
        )

    def send_msg(k, carry):
        msg_copy(k).start()
        return carry

    lax.fori_loop(1, devices, send_msg, 0)
    msgs_ref[pl.ds(me, 1)] = msg[0:1]

    def finish(k, carry):
        row_copy(k).wait()
        msg_copy(k).wait()
        return carry

    lax.fori_loop(1, devices, finish, 0)


def place_kernel(clips_ref, targets_ref, msgs_ref, arrived_ref, gain_ref, bias_ref,
                 features_ref, act_ref, first_ref, last_ref, mean_s, inv_s):
    rows, channels = features_ref.shape
    width = channels // GROUPS
    sums = msgs_ref[:, 1, :]
    squares = msgs_ref[:, 2, :]
    counts = msgs_ref[:, 3, :]
    total = jnp.sum(counts, axis=0, keepdims=True)
    mean = jnp.sum(sums, axis=0, keepdims=True) / total
    off = sums / jnp.maximum(counts, 1.0) - mean
    var = jnp.sum(squares + counts * (off * off), axis=0, keepdims=True) / total
    inv = 1.0 / jnp.sqrt(var + 1e-06)
    spread = group_matrix_t(channels, width)
    own_lanes = clip_lanes()
    mean_s[...] = dot_exact(jnp.where(own_lanes, mean, 0.0), spread)
    inv_s[...] = dot_exact(jnp.where(own_lanes, inv, 0.0), spread)
    first_frame = lax.axis_index("frame") * FR_DEV
    plane = HR * WCOL
    first_ref[...] = jnp.zeros_like(first_ref)
    last_ref[...] = jnp.zeros_like(last_ref)
    arrived = decode(arrived_ref[...])
    hi = arrived.astype(BF)
    rest = (arrived - hi.astype(F32)).astype(BF)
    for t in range(FR_DEV):
        pick = (iota((plane, targets_ref.shape[1]), 0) + t * plane == targets_ref[...]).astype(F32).astype(BF)
        x = dot(pick, hi) + dot(pick, rest)
        features_ref[pl.ds(t * plane, plane), :] = x
        c = clips_ref[first_frame + t]
        normed = (x - mean_s[pl.ds(c, 1), :]) * inv_s[pl.ds(c, 1), :]
        v = normed * gain_ref[...] + bias_ref[...]
        act = v / (1.0 + jnp.exp(-v))
        for h in range(HR):
            slab = act[h * WCOL : (h + 1) * WCOL]
            act_ref[t, h] = slab.astype(BF)
            rounded = slab.astype(BF).astype(F32)
            first_ref[h, t : t + 1, :] = rounded[0:1]
            last_ref[h, t : t + 1, :] = rounded[WCOL - 1 : WCOL]


def halo_kernel(sizes, act_ref, first_ref, last_ref, x_ref, cl_ref, cr_ref, own_sem, send_sem, recv_sem):
    n_src, n_frame, n_tile = sizes
    s, f, t = lax.axis_index("src"), lax.axis_index("frame"), lax.axis_index("tile")
    x_ref[0:2] = jnp.zeros_like(x_ref[0:2])
    for edge in (0, HR + 1):
        x_ref[2:, edge] = jnp.zeros_like(x_ref[2:, edge])
    cl_ref[...] = jnp.zeros_like(cl_ref)
    cr_ref[...] = jnp.zeros_like(cr_ref)

    moves = [(ds, df, dt) for df in (0, 1) for dt in (0, -1, 1) for ds in (0, -1, 1)][1:]

    def inside(ds, df, dt):
        return ((s + ds >= 0) & (s + ds < n_src) & (f + df >= 0) & (f + df < n_frame)
                & (t + dt >= 0) & (t + dt < n_tile))

    barrier = pltpu.get_barrier_semaphore()
    heard = jnp.int32(0)
    for ds, df, dt in moves:
        @pl.when(inside(-ds, -df, -dt))
        def _():
            pl.semaphore_signal(barrier, inc=1, device_id=(s - ds, f - df, t - dt), device_id_type=MESH)

        heard = heard + inside(ds, df, dt).astype(jnp.int32)
    pl.semaphore_wait(barrier, heard)

    def copy(i, move):
        ds, df, dt = move
        from_h, to_h, count = {0: (0, 1, HR), 1: (HR - 1, 0, 1), -1: (0, HR + 1, 1)}[dt]
        if ds == 0:
            from_t, to_t, frames = (0, 2, FR_DEV) if df == 0 else (FR_DEV - 2, 0, 2)
            src = act_ref.at[pl.ds(from_t, frames), pl.ds(from_h, count)]
            dst = x_ref.at[pl.ds(to_t, frames), pl.ds(to_h, count)]
        else:
            src = (last_ref if ds == 1 else first_ref).at[pl.ds(from_h, count)]
            dst = (cl_ref if ds == 1 else cr_ref).at[df, pl.ds(to_h, count)]
        return pltpu.make_async_remote_copy(
            src_ref=src, dst_ref=dst, send_sem=send_sem.at[i], recv_sem=recv_sem.at[i],
            device_id=(s + ds, f + df, t + dt), device_id_type=MESH,
        )

    for i, move in enumerate(moves):
        @pl.when(inside(*move))
        def _(i=i, move=move):
            copy(i, move).start()
    own = pltpu.make_async_copy(act_ref, x_ref.at[pl.ds(2, FR_DEV), pl.ds(1, HR)], own_sem)
    own.start()
    own.wait()
    for i, move in enumerate(moves):
        @pl.when(inside(*move))
        def _(i=i, move=move):
            copy(i, move).wait_send()

        @pl.when(inside(-move[0], -move[1], -move[2]))
        def _(i=i, move=move):
            copy(i, move).wait_recv()


def conv_kernel(clips_ref, x_ref, cl_ref, cr_ref, w_ref, features_ref, bias_ref, out_ref, xs, acc):
    step = pl.program_id(0)
    channels = x_ref.shape[-1]
    plane = HR * WCOL
    first_frame = lax.axis_index("frame") * FR_DEV
    a, b = step // 3, step % 3

    @pl.when(step == 0)
    def _():
        row = iota((WCOL, channels), 0)

        def widen(h, carry):
            for t in range(FR_DEV + 2):
                here = x_ref[t, h]
                wide = here.astype(F32)
                part, line = (1, FR_DEV - 2 + t) if t < 2 else (0, t - 2)
                left = cl_ref[part, h][line : line + 1]
                right = cr_ref[part, h][line : line + 1]
                xs[t, h, :, 0:channels] = jnp.where(row == 0, left, pltpu.roll(wide, 1, 0)).astype(BF)
                xs[t, h, :, channels : 2 * channels] = here
                xs[t, h, :, 2 * channels :] = jnp.where(
                    row == WCOL - 1, right, pltpu.roll(wide, WCOL - 1, 0)
                ).astype(BF)
            return carry

        lax.fori_loop(0, HR + 2, widen, 0)
        acc[...] = jnp.zeros_like(acc)

    for t in range(0, FR_DEV, 2):
        lhs = xs[pl.ds(a + t, 2), pl.ds(b, HR)].reshape(2 * plane, 3 * channels)
        part = dot(lhs, w_ref[0])
        for u in range(2):
            frame = first_frame + t + u
            source = frame - 2 + a
            same = (source >= 0) & (clips_ref[jnp.maximum(source, 0)] == clips_ref[frame])
            at = pl.ds((t + u) * plane, plane)
            acc[at, :] += jnp.where(same, part[u * plane : (u + 1) * plane], 0.0)

    @pl.when(step == 8)
    def _():
        for t in range(FR_DEV):
            at = pl.ds(t * plane, plane)
            y = features_ref[at, :] + acc[at, :] + bias_ref[...]
            out_ref[t] = y.astype(BF).reshape(HR, WCOL, channels)


def shards(feats, row_map, clip_ids, norm_gain, norm_bias, conv_weight, conv_bias):
    rows, channels = feats.shape
    sizes = tuple(lax.axis_size(name) for name in ("src", "frame", "tile"))
    n_src, n_frame, n_tile = sizes
    devices = n_src * n_frame * n_tile
    block = (rows // devices + 15) // 16 * 16
    me = (lax.axis_index("src") * n_frame + lax.axis_index("frame")) * n_tile + lax.axis_index("tile")
    owner = row_map // rows
    slot = row_map % rows
    frame = owner // n_tile % n_frame * FR_DEV + slot // (HR * WCOL)
    frames = jnp.arange(clip_ids.shape[0], dtype=jnp.int32)
    clip = jnp.sum(jnp.where(frames[:, None] == frame[None, :], clip_ids[:, None], 0), axis=0)
    info = jnp.stack([(owner - me) % devices, slot // 32, slot % 32, clip])
    vmem = pl.BlockSpec(memory_space=pltpu.VMEM)
    smem = pl.BlockSpec(memory_space=pltpu.SMEM)
    dma = pltpu.SemaphoreType.DMA
    arrived, msgs = pl.pallas_call(
        functools.partial(reshard_kernel, sizes, block),
        out_shape=(
            jax.ShapeDtypeStruct((devices * block, channels), CODE),
            jax.ShapeDtypeStruct((devices, 8, 128), F32),
        ),
        in_specs=[vmem] * 2,
        out_specs=(vmem, vmem),
        scratch_shapes=[
            pltpu.VMEM((devices * block, channels), CODE),
            pltpu.VMEM((devices, 8, 128), F32),
            dma((devices,)),
            dma((devices,)),
            dma((devices,)),
            dma((devices,)),
        ],
        compiler_params=pltpu.CompilerParams(
            collective_id=0, has_side_effects=True, vmem_limit_bytes=VMEM_LIMIT
        ),
        name="reshard",
    )(info, feats)
    targets = msgs[:, 0, :block].reshape(1, devices * block).astype(jnp.int32)
    edge = jax.ShapeDtypeStruct((HR, 8, channels), F32)
    features, act, first, last = pl.pallas_call(
        place_kernel,
        out_shape=(
            jax.ShapeDtypeStruct((rows, channels), F32),
            jax.ShapeDtypeStruct((FR_DEV, HR, WCOL, channels), BF),
            edge,
            edge,
        ),
        in_specs=[smem] + [vmem] * 5,
        out_specs=(vmem,) * 4,
        scratch_shapes=[pltpu.VMEM((8, channels), F32)] * 2,
        compiler_params=pltpu.CompilerParams(vmem_limit_bytes=VMEM_LIMIT),
        name="place",
    )(clip_ids, targets, msgs, arrived, norm_gain[None], norm_bias[None])
    beside = jax.ShapeDtypeStruct((2, HR + 2, 8, channels), F32)
    x, left, right = pl.pallas_call(
        functools.partial(halo_kernel, sizes),
        out_shape=(
            jax.ShapeDtypeStruct((FR_DEV + 2, HR + 2, WCOL, channels), BF),
            beside,
            beside,
        ),
        in_specs=[vmem] * 3,
        out_specs=(vmem,) * 3,
        scratch_shapes=[dma, dma((17,)), dma((17,))],
        compiler_params=pltpu.CompilerParams(
            collective_id=1, has_side_effects=True, vmem_limit_bytes=VMEM_LIMIT
        ),
        name="halo",
    )(act, first, last)
    whole = lambda *shape: pl.BlockSpec(shape, lambda i: (0,) * len(shape))
    return pl.pallas_call(
        conv_kernel,
        grid=(9,),
        out_shape=jax.ShapeDtypeStruct((FR_DEV, HR, WCOL, channels), BF),
        in_specs=[
            smem,
            vmem,
            vmem,
            vmem,
            pl.BlockSpec((1, 3 * channels, channels), lambda i: (i, 0, 0)),
            vmem,
            vmem,
        ],
        out_specs=whole(FR_DEV, HR, WCOL, channels),
        scratch_shapes=[
            pltpu.VMEM((FR_DEV + 2, HR + 2, WCOL, 3 * channels), BF),
            pltpu.VMEM((rows, channels), F32),
        ],
        compiler_params=pltpu.CompilerParams(vmem_limit_bytes=VMEM_LIMIT),
        name="conv",
    )(clip_ids, x, left, right, conv_weight.reshape(9, 3 * channels, channels), features, conv_bias[None])


def solution(mesh):
    placed = (
        P(("src", "frame", "tile"), None),
        P(("src", "frame", "tile")),
        P(),
        P(),
        P(),
        P(),
        P(),
    )
    return jax.shard_map(
        shards,
        mesh=mesh,
        in_specs=placed,
        out_specs=P("frame", "tile", "src", None),
        check_vma=False,
    )
```

time: 305 us -> 122 us (0.40)
  Pallas kernels: 0 us -> 116 us
  blocking collectives: 79 us -> 0 us
  waiting for transfers between devices: 72.6 us -> 0 us
  local copies, waits for them, and re-layouts: 59.2 us -> 0.7 us
  matrix products: 31.9 us -> 0 us
  other arithmetic: 32.7 us -> 3.08 us
  starting transfers between devices: 28.2 us -> 0 us
    pallas_call x0 -> x4, Pallas kernels: none -> 116 us  [the longest x1 53 us: shards(): pl.pallas_call(functools.partial(reshard_kernel, sizes, block), out_shape...]
    psum x2 -> x0, blocking collectives: 79 us -> none  [the longest x1 40.2 us: shards(): clip_mean = lax.psum(local_sum, ('src', 'frame', 'tile')) / counts[:, None]]
    all_to_all x2 -> x0, waiting for transfers between devices: 64.6 us -> none  [the longest x1 62.9 us: shards(): lax.all_to_all(outgoing.reshape(devices, per_pair, channels), ('src', 'fr...]
    dot_general x13 -> x0, matrix products: 31.9 us -> none  [the longest x9 31 us: shards(): jnp.dot(stacked.reshape(-1, 3 * channels), kernel, preferred_element_type...]
    slice x6 -> x0, local copies, waits for them, and re-layouts: 25.9 us -> none  [the longest x3 16.2 us: shards(): padded[tap_time:tap_time + FR_DEV, tap_high:tap_high + HR, tap_wide:tap_w...]
    gather x4 -> x0, local copies, waits for them, and re-layouts: 20.7 us -> none  [the longest x1 8.39 us: shards(): slot_ids = (row_map % local_rows)[ordering]]
    ppermute x5 -> x0, starting transfers between devices: 16.9 us -> none  [the longest x2 9.97 us: with_halo(): before = lax.ppermute(last, axis, up)]
    all_to_all x2 -> x0, starting transfers between devices: 11.3 us -> none  [the longest x1 7.1 us: shards(): lax.all_to_all(slot_ids.reshape(devices, per_pair), ('src', 'frame', 'til...]
  transfers between devices with their start and end apart: 7 -> 0, of which waited for: 5 -> 0; matrix products, arithmetic and copies ran while one was open for 8% -> 0% of each run, Pallas kernels for 0% -> 0%
where the time goes in v1:
time: 122 us; the launch traced here: 120 us
  Pallas kernels  116 us (95%)
  other arithmetic  3.08 us (3%)
    pallas_call x1, Pallas kernels, shards(): pl.pallas_call(functools.partial(reshard_kernel, sizes, block), out_shape...  53 us
    pallas_call x1, Pallas kernels, shards(): pl.pallas_call(conv_kernel, grid=(9,), out_shape=jax.ShapeDtypeStruct((FR...  29.9 us
    pallas_call x1, Pallas kernels, shards(): pl.pallas_call(functools.partial(halo_kernel, sizes), out_shape=(jax.Shap...  22.4 us
    pallas_call x1, Pallas kernels, shards(): pl.pallas_call(place_kernel, out_shape=(jax.ShapeDtypeStruct((rows, chann...  11.2 us

profile of v1, /device:TPU:1, one launch (start us, length us, event | category | flops | bytes accessed | tf_op | source)
XLA Modules:
  0.0 120.3 jit_solution(14213492036675441568)
XLA Ops:
  0.0 0.7 add_select_fusion.6
  0.8 0.7 select_reduce_fusion
  1.5 0.6 pad_add_fusion.info_ref
  2.2 53.0 %reshard.1 = (s16[1536,512]{1,0:T(8,128)(2,1)}, f32[32,8,128]{2,1,0:T(8,128)}) custom-call(s32[4,1536]{1,0:T(4,128)} %pad_add_fusion.info_ref, f32[1536,512]{1,0:T(8,128)} %feats_ref.1), custom_call_target="tpu_custom_call" | custom-call | tf_op jit(solution)/shard_map/reshard/pallas_call | solution.py:359
  55.2 1.0 convert_reduce_fusion
  56.2 0.7 convert_element_type.6.targets_ref
  56.8 11.2 %place.1 = (f32[1536,512]{1,0:T(8,128)}, bf16[6,8,32,512]{3,2,1,0:T(8,128)(2,1)}, f32[8,8,512]{2,1,0:T(8,128)}, f32[8,8,512]{2,1,0:T(8,128)}) custom-call(s32[12]{0:T(128)} %clips_ref.3, s32[1,1536]{1,0:T(1,128)} %convert_element_type.6.targets_ref, f32[32,8,128]{2,1,0:T(8,128)} %get-tuple-element.14.msgs_ref, ...), custom_call_target="tpu_custom_call" | custom-call | tf_op jit(solution)/shard_map/place/pallas_call | solution.py:382
  68.0 22.4 %halo.1 = (bf16[8,10,32,512]{3,2,1,0:T(8,128)(2,1)}, f32[2,10,8,512]{3,2,1,0:T(8,128)}, f32[2,10,8,512]{3,2,1,0:T(8,128)}) custom-call(bf16[6,8,32,512]{3,2,1,0:T(8,128)(2,1)} %get-tuple-element.16.act_ref, f32[8,8,512]{2,1,0:T(8,128)} %get-tuple-element.17.first_ref, f32[8,8,512]{2,1,0:T(8,128)} %get-tuple-element.18.last_ref), custom_call_target="tpu_custom_call" | custom-call | tf_op jit(solution)/shard_map/halo/pallas_call | solution.py:397
  90.4 29.9 %conv.1 = bf16[6,8,32,512]{3,2,1,0:T(8,128)(2,1)} custom-call(s32[12]{0:T(128)} %clips_ref.3, bf16[8,10,32,512]{3,2,1,0:T(8,128)(2,1)} %get-tuple-element.19.x_ref, f32[2,10,8,512]{3,2,1,0:T(8,128)} %get-tuple-element.20.cl_ref, f32[2,10,8,512]{3,2,1,0:T(8,128)} %get-tuple-element.21.cr_ref, bf16[9,1536,512]{2,1,0:T(8,128)(2,1)} %bitcast.4, ...), custom_call_target="tpu_custom_call" | custom-call | tf_op jit(solution)/shard_map/conv/pallas_call | solution.py:413
  (4 shorter events, 0.0 us)

commit v2 on v1

--- a/solution.py
+++ b/solution.py
@@ -199,7 +199,7 @@
 
 
 def place_kernel(clips_ref, targets_ref, msgs_ref, arrived_ref, gain_ref, bias_ref,
-                 features_ref, act_ref, first_ref, last_ref, mean_s, inv_s):
+                 features_ref, act_ref, first_ref, last_ref, firstp_ref, lastp_ref, mean_s, inv_s):
     rows, channels = features_ref.shape
     width = channels // GROUPS
     sums = msgs_ref[:, 1, :]
@@ -235,18 +235,33 @@
             rounded = slab.astype(BF).astype(F32)
             first_ref[h, t : t + 1, :] = rounded[0:1]
             last_ref[h, t : t + 1, :] = rounded[WCOL - 1 : WCOL]
-
-
-def halo_kernel(sizes, act_ref, first_ref, last_ref, x_ref, cl_ref, cr_ref, own_sem, send_sem, recv_sem):
+            if t >= FR_DEV - 2:
+                u = t - (FR_DEV - 2)
+                firstp_ref[u, h : h + 1, :] = rounded[0:1]
+                lastp_ref[u, h : h + 1, :] = rounded[WCOL - 1 : WCOL]
+
+
+def decode_kernel(sizes, clips_ref, act_ref, first_ref, last_ref, firstp_ref, lastp_ref, features_ref, bias_ref,
+                  w_ref, out_ref, xs, acc, weights, prev, edge, col, corner, colp, cornerp,
+                  w_sem, send_sem, recv_sem):
     n_src, n_frame, n_tile = sizes
     s, f, t = lax.axis_index("src"), lax.axis_index("frame"), lax.axis_index("tile")
-    x_ref[0:2] = jnp.zeros_like(x_ref[0:2])
-    for edge in (0, HR + 1):
-        x_ref[2:, edge] = jnp.zeros_like(x_ref[2:, edge])
-    cl_ref[...] = jnp.zeros_like(cl_ref)
-    cr_ref[...] = jnp.zeros_like(cr_ref)
-
-    moves = [(ds, df, dt) for df in (0, 1) for dt in (0, -1, 1) for ds in (0, -1, 1)][1:]
+    channels = act_ref.shape[-1]
+    plane = HR * WCOL
+
+    def weight_copy(i):
+        return pltpu.make_async_copy(w_ref.at[i], weights.at[i], w_sem.at[i])
+
+    taps_order = [1, 4, 7, 0, 3, 6, 2, 5, 8]
+    for i in taps_order:
+        weight_copy(i).start()
+    for ref in (prev, edge, col, corner, colp, cornerp):
+        ref[...] = jnp.zeros_like(ref)
+
+    moves = [(ds, 0, 0) for ds in (-1, 1)]
+    moves += [(0, 1, 0)]
+    moves += [(ds, 0, dt) for dt in (-1, 1) for ds in (0, -1, 1)]
+    moves += [(ds, 1, dt) for dt in (0, -1, 1) for ds in (0, -1, 1)][1:]
 
     def inside(ds, df, dt):
         return ((s + ds >= 0) & (s + ds < n_src) & (f + df >= 0) & (f + df < n_frame)
@@ -260,18 +275,30 @@
             pl.semaphore_signal(barrier, inc=1, device_id=(s - ds, f - df, t - dt), device_id_type=MESH)
 
         heard = heard + inside(ds, df, dt).astype(jnp.int32)
+
+    for u in range(FR_DEV):
+        at = pl.ds(u * plane, plane)
+        acc[at, :] = features_ref[at, :] + bias_ref[...]
     pl.semaphore_wait(barrier, heard)
 
     def copy(i, move):
         ds, df, dt = move
-        from_h, to_h, count = {0: (0, 1, HR), 1: (HR - 1, 0, 1), -1: (0, HR + 1, 1)}[dt]
-        if ds == 0:
-            from_t, to_t, frames = (0, 2, FR_DEV) if df == 0 else (FR_DEV - 2, 0, 2)
-            src = act_ref.at[pl.ds(from_t, frames), pl.ds(from_h, count)]
-            dst = x_ref.at[pl.ds(to_t, frames), pl.ds(to_h, count)]
+        row = HR - 1 if dt == 1 else 0
+        end = 0 if dt == 1 else 1
+        side = 0 if ds == 1 else 1
+        if ds == 0 and df == 0:
+            src, dst = act_ref.at[:, row], edge.at[end]
+        elif ds == 0:
+            src = act_ref.at[pl.ds(FR_DEV - 2, 2), pl.ds(0, HR)] if dt == 0 else act_ref.at[pl.ds(FR_DEV - 2, 2), row]
+            dst = prev.at[:, pl.ds(1, HR)] if dt == 0 else prev.at[:, (HR + 1) * end]
+        elif df == 0:
+            ref = last_ref if ds == 1 else first_ref
+            src, dst = (ref, col.at[side]) if dt == 0 else (ref.at[row], corner.at[side, end])
         else:
-            src = (last_ref if ds == 1 else first_ref).at[pl.ds(from_h, count)]
-            dst = (cl_ref if ds == 1 else cr_ref).at[df, pl.ds(to_h, count)]
+            if dt == 0:
+                src, dst = lastp_ref if ds == 1 else firstp_ref, colp.at[side]
+            else:
+                src, dst = (last_ref if ds == 1 else first_ref).at[row], cornerp.at[side, end]
         return pltpu.make_async_remote_copy(
             src_ref=src, dst_ref=dst, send_sem=send_sem.at[i], recv_sem=recv_sem.at[i],
             device_id=(s + ds, f + df, t + dt), device_id_type=MESH,
@@ -281,63 +308,98 @@
         @pl.when(inside(*move))
         def _(i=i, move=move):
             copy(i, move).start()
-    own = pltpu.make_async_copy(act_ref, x_ref.at[pl.ds(2, FR_DEV), pl.ds(1, HR)], own_sem)
-    own.start()
-    own.wait()
+
+    def arrive(lo, hi):
+        for i, move in list(enumerate(moves))[lo:hi]:
+            @pl.when(inside(-move[0], -move[1], -move[2]))
+            def _(i=i, move=move):
+                copy(i, move).wait_recv()
+
+    first_frame = f * FR_DEV
+
+    def add(part, a, lo):
+        for j in range(part.shape[0] // plane):
+            here = part[j * plane : (j + 1) * plane]
+            at = pl.ds((lo + j) * plane, plane)
+            if a < 2:
+                frame = first_frame + lo + j
+                source = frame - 2 + a
+                same = (source >= 0) & (clips_ref[jnp.maximum(source, 0)] == clips_ref[frame])
+                here = jnp.where(same, here, 0.0)
+            acc[at, :] += here
+
+    groups = [(2, 0, 3), (2, 3, 3), (1, 1, 3), (1, 4, 2), (0, 2, 2), (0, 4, 2)]
+    mid_lanes = slice(channels, 2 * channels)
+    for a, lo, n in groups:
+        if lo in (0, 1, 2):
+            weight_copy(3 * a + 1).wait()
+        u = lo - 2 + a
+        lhs = act_ref[u : u + n].reshape(n * plane, channels)
+        add(dot(lhs, weights[3 * a + 1, mid_lanes]), a, lo)
+
+    rows32 = iota((WCOL, channels), 0)
+
+    def widen(u, h, here, left, right):
+        wide = here.astype(F32)
+        xs[u, h, :, 0:channels] = jnp.where(rows32 == 0, left, pltpu.roll(wide, 1, 0)).astype(BF)
+        xs[u, h, :, channels : 2 * channels] = here
+        xs[u, h, :, 2 * channels :] = jnp.where(
+            rows32 == WCOL - 1, right, pltpu.roll(wide, WCOL - 1, 0)
+        ).astype(BF)
+
+    arrive(0, 2)
+
+    def widen_own(h, carry):
+        for u in range(FR_DEV):
+            widen(u + 2, h + 1, act_ref[u, h], col[0, h, u : u + 1], col[1, h, u : u + 1])
+        return carry
+
+    lax.fori_loop(0, HR, widen_own, 0)
+
+    def taken(u, n, b, lanes):
+        return xs[u : u + n, b : b + HR, :, lanes].reshape(n * plane, -1)
+
+    for a, lo, n in groups:
+        u = lo + a
+        w = weights.at[3 * a + 1]
+        part = dot(taken(u, n, 1, slice(0, channels)), w[0:channels])
+        part = part + dot(taken(u, n, 1, slice(2 * channels, 3 * channels)), w[2 * channels : 3 * channels])
+        add(part, a, lo)
+
+    arrive(3, 9)
+    for end, h in ((0, 0), (1, HR + 1)):
+        for u in range(FR_DEV):
+            widen(u + 2, h, edge[end, u], corner[0, end, u : u + 1], corner[1, end, u : u + 1])
+    for i in (0, 3, 6, 2, 5, 8):
+        weight_copy(i).wait()
+    every = slice(0, 3 * channels)
+    for a, lo, n in groups:
+        u = lo + a
+        part = dot(taken(u, n, 0, every), weights[3 * a]) + dot(taken(u, n, 2, every), weights[3 * a + 2])
+        add(part, a, lo)
+
+    arrive(2, 3)
+    arrive(9, len(moves))
+    for u in range(2):
+        line = FR_DEV - 2 + u
+        for h in range(HR + 2):
+            if 0 < h < HR + 1:
+                left, right = colp[0, u, h - 1 : h], colp[1, u, h - 1 : h]
+            else:
+                end = h // (HR + 1)
+                left, right = cornerp[0, end, line : line + 1], cornerp[1, end, line : line + 1]
+            widen(u, h, prev[u, h], left, right)
+    for a, n in ((0, 2), (1, 1)):
+        part = dot(taken(a, n, 0, every), weights[3 * a])
+        part = part + dot(taken(a, n, 1, every), weights[3 * a + 1])
+        part = part + dot(taken(a, n, 2, every), weights[3 * a + 2])
+        add(part, a, 0)
+    for u in range(FR_DEV):
+        out_ref[u] = acc[pl.ds(u * plane, plane), :].astype(BF).reshape(HR, WCOL, channels)
     for i, move in enumerate(moves):
         @pl.when(inside(*move))
         def _(i=i, move=move):
             copy(i, move).wait_send()
-
-        @pl.when(inside(-move[0], -move[1], -move[2]))
-        def _(i=i, move=move):
-            copy(i, move).wait_recv()
-
-
-def conv_kernel(clips_ref, x_ref, cl_ref, cr_ref, w_ref, features_ref, bias_ref, out_ref, xs, acc):
-    step = pl.program_id(0)
-    channels = x_ref.shape[-1]
-    plane = HR * WCOL
-    first_frame = lax.axis_index("frame") * FR_DEV
-    a, b = step // 3, step % 3
-
-    @pl.when(step == 0)
-    def _():
-        row = iota((WCOL, channels), 0)
-
-        def widen(h, carry):
-            for t in range(FR_DEV + 2):
-                here = x_ref[t, h]
-                wide = here.astype(F32)
-                part, line = (1, FR_DEV - 2 + t) if t < 2 else (0, t - 2)
-                left = cl_ref[part, h][line : line + 1]
-                right = cr_ref[part, h][line : line + 1]
-                xs[t, h, :, 0:channels] = jnp.where(row == 0, left, pltpu.roll(wide, 1, 0)).astype(BF)
-                xs[t, h, :, channels : 2 * channels] = here
-                xs[t, h, :, 2 * channels :] = jnp.where(
-                    row == WCOL - 1, right, pltpu.roll(wide, WCOL - 1, 0)
-                ).astype(BF)
-            return carry
-
-        lax.fori_loop(0, HR + 2, widen, 0)
-        acc[...] = jnp.zeros_like(acc)
-
-    for t in range(0, FR_DEV, 2):
-        lhs = xs[pl.ds(a + t, 2), pl.ds(b, HR)].reshape(2 * plane, 3 * channels)
-        part = dot(lhs, w_ref[0])
-        for u in range(2):
-            frame = first_frame + t + u
-            source = frame - 2 + a
-            same = (source >= 0) & (clips_ref[jnp.maximum(source, 0)] == clips_ref[frame])
-            at = pl.ds((t + u) * plane, plane)
-            acc[at, :] += jnp.where(same, part[u * plane : (u + 1) * plane], 0.0)
-
-    @pl.when(step == 8)
-    def _():
-        for t in range(FR_DEV):
-            at = pl.ds(t * plane, plane)
-            y = features_ref[at, :] + acc[at, :] + bias_ref[...]
-            out_ref[t] = y.astype(BF).reshape(HR, WCOL, channels)
 
 
 def shards(feats, row_map, clip_ids, norm_gain, norm_bias, conv_weight, conv_bias):
@@ -379,58 +441,48 @@
     )(info, feats)
     targets = msgs[:, 0, :block].reshape(1, devices * block).astype(jnp.int32)
     edge = jax.ShapeDtypeStruct((HR, 8, channels), F32)
-    features, act, first, last = pl.pallas_call(
+    edge_p = jax.ShapeDtypeStruct((2, HR, channels), F32)
+    features, act, first, last, firstp, lastp = pl.pallas_call(
         place_kernel,
         out_shape=(
             jax.ShapeDtypeStruct((rows, channels), F32),
             jax.ShapeDtypeStruct((FR_DEV, HR, WCOL, channels), BF),
             edge,
             edge,
+            edge_p,
+            edge_p,
         ),
         in_specs=[smem] + [vmem] * 5,
-        out_specs=(vmem,) * 4,
+        out_specs=(vmem,) * 6,
         scratch_shapes=[pltpu.VMEM((8, channels), F32)] * 2,
         compiler_params=pltpu.CompilerParams(vmem_limit_bytes=VMEM_LIMIT),
         name="place",
     )(clip_ids, targets, msgs, arrived, norm_gain[None], norm_bias[None])
-    beside = jax.ShapeDtypeStruct((2, HR + 2, 8, channels), F32)
-    x, left, right = pl.pallas_call(
-        functools.partial(halo_kernel, sizes),
-        out_shape=(
-            jax.ShapeDtypeStruct((FR_DEV + 2, HR + 2, WCOL, channels), BF),
-            beside,
-            beside,
-        ),
-        in_specs=[vmem] * 3,
-        out_specs=(vmem,) * 3,
-        scratch_shapes=[dma, dma((17,)), dma((17,))],
+    return pl.pallas_call(
+        functools.partial(decode_kernel, sizes),
+        out_shape=jax.ShapeDtypeStruct((FR_DEV, HR, WCOL, channels), BF),
+        in_specs=[smem] + [vmem] * 7 + [pl.BlockSpec(memory_space=pl.ANY)],
+        out_specs=vmem,
+        scratch_shapes=[
+            pltpu.VMEM((FR_DEV + 2, HR + 2, WCOL, 3 * channels), BF),
+            pltpu.VMEM((rows, channels), F32),
+            pltpu.VMEM((9, 3 * channels, channels), BF),
+            pltpu.VMEM((2, HR + 2, WCOL, channels), BF),
+            pltpu.VMEM((2, FR_DEV, WCOL, channels), BF),
+            pltpu.VMEM((2, HR, 8, channels), F32),
+            pltpu.VMEM((2, 2, 8, channels), F32),
+            pltpu.VMEM((2, 2, HR, channels), F32),
+            pltpu.VMEM((2, 2, 8, channels), F32),
+            dma((9,)),
+            dma((17,)),
+            dma((17,)),
+        ],
         compiler_params=pltpu.CompilerParams(
             collective_id=1, has_side_effects=True, vmem_limit_bytes=VMEM_LIMIT
         ),
-        name="halo",
-    )(act, first, last)
-    whole = lambda *shape: pl.BlockSpec(shape, lambda i: (0,) * len(shape))
-    return pl.pallas_call(
-        conv_kernel,
-        grid=(9,),
-        out_shape=jax.ShapeDtypeStruct((FR_DEV, HR, WCOL, channels), BF),
-        in_specs=[
-            smem,
-            vmem,
-            vmem,
-            vmem,
-            pl.BlockSpec((1, 3 * channels, channels), lambda i: (i, 0, 0)),
-            vmem,
-            vmem,
-        ],
-        out_specs=whole(FR_DEV, HR, WCOL, channels),
-        scratch_shapes=[
-            pltpu.VMEM((FR_DEV + 2, HR + 2, WCOL, 3 * channels), BF),
-            pltpu.VMEM((rows, channels), F32),
-        ],
-        compiler_params=pltpu.CompilerParams(vmem_limit_bytes=VMEM_LIMIT),
-        name="conv",
-    )(clip_ids, x, left, right, conv_weight.reshape(9, 3 * channels, channels), features, conv_bias[None])
+        name="halo_conv",
+    )(clip_ids, act, first, last, firstp, lastp, features, conv_bias[None],
+      conv_weight.reshape(9, 3 * channels, channels))
 
 
 def solution(mesh):

time: 122 us -> 102 us (0.84); the launches traced: 120 us -> 102 us
  Pallas kernels: 116 us -> 95 us
  local copies, waits for them, and re-layouts: 0.7 us -> 3.42 us
    pallas_call x2 -> x1, Pallas kernels: 52.3 us -> 30.8 us  [shards(): pl.pallas_call(functools.partial(decode_kernel, sizes), out_shape=jax.Sha...]
    unnamed x0 -> x1, local copies, waits for them, and re-layouts: none -> 2.73 us
where the time goes in v2:
time: 102 us
  Pallas kernels  95 us (93%)
  local copies, waits for them, and re-layouts  3.42 us (3%)
  other arithmetic  3.08 us (3%)
    pallas_call x1, Pallas kernels, shards(): pl.pallas_call(functools.partial(reshard_kernel, sizes, block), out_shape...  53 us
    pallas_call x1, Pallas kernels, shards(): pl.pallas_call(functools.partial(decode_kernel, sizes), out_shape=jax.Sha...  30.8 us
    pallas_call x1, Pallas kernels, shards(): pl.pallas_call(place_kernel, out_shape=(jax.ShapeDtypeStruct((rows, chann...  11.2 us
    unnamed x1, local copies, waits for them, and re-layouts  2.73 us

profile of v2, /device:TPU:1, one launch (start us, length us, event | category | flops | bytes accessed | tf_op | source)
XLA Modules:
  0.0 101.6 jit_solution(8888475318851261737)
XLA Ops:
  0.0 0.7 add_select_fusion.6
  0.8 0.7 select_reduce_fusion
  1.5 0.6 pad_add_fusion.info_ref
  2.2 53.0 %reshard.1 = (s16[1536,512]{1,0:T(8,128)(2,1)}, f32[32,8,128]{2,1,0:T(8,128)}) custom-call(s32[4,1536]{1,0:T(4,128)} %pad_add_fusion.info_ref, f32[1536,512]{1,0:T(8,128)} %feats_ref.1), custom_call_target="tpu_custom_call" | custom-call | tf_op jit(solution)/shard_map/reshard/pallas_call | solution.py:421
  55.2 1.0 convert_reduce_fusion
  56.2 0.7 convert_element_type.6.targets_ref
  56.9 11.2 %place.1 = (f32[1536,512]{1,0:T(8,128)}, bf16[6,8,32,512]{3,2,1,0:T(8,128)(2,1)}, f32[8,8,512]{2,1,0:T(8,128)}, f32[8,8,512]{2,1,0:T(8,128)}, f32[2,8,512]{2,1,0:T(8,128)}, /*index=5*/f32[2,8,512]{2,1,0:T(8,128)}) custom-call(s32[12]{0:T(128)} %clips_ref.3, s32[1,1536]{1,0:T(1,128)} %convert_element_type.6.targets_ref, ...), custom_call_target="tpu_custom_call" | custom-call | tf_op jit(solution)/shard_map/place/pallas_call | solution.py:445
  68.1 30.8 %halo_conv.1 = bf16[6,8,32,512]{3,2,1,0:T(8,128)(2,1)} custom-call(s32[12]{0:T(128)} %clips_ref.3, bf16[6,8,32,512]{3,2,1,0:T(8,128)(2,1)} %get-tuple-element.15.act_ref, f32[8,8,512]{2,1,0:T(8,128)} %get-tuple-element.16.first_ref, f32[8,8,512]{2,1,0:T(8,128)} %get-tuple-element.17.last_ref, f32[2,8,512]{2,1,0:T(8,128)} %get-tuple-element.18.firstp_ref, ...), custom_call_target="tpu_custom_call" | custom-call | tf_op jit(solution)/shard_map/halo_conv/pallas_call | solution.py:461
  98.8 2.7 %copy.9 = bf16[6,8,32,512]{3,2,1,0:T(8,128)(2,1)} copy(bf16[6,8,32,512]{3,2,1,0:T(8,128)(2,1)} %halo_conv.1) | data formatting | bytes 3145728
  (4 shorter events, 0.0 us)

commit v3 on v2

--- a/solution.py
+++ b/solution.py
@@ -69,8 +69,10 @@
     return iota((8, 128), 1) // GROUPS == iota((8, 128), 0)
 
 
-def reshard_kernel(sizes, block, info_ref, feats_ref, arrived_ref, msgs_ref, packed, msg,
-                   send_sem, recv_sem, msend_sem, mrecv_sem):
+def reshard_kernel(sizes, block, clips_ref, info_ref, feats_ref, gain_ref, bias_ref,
+                   features_ref, act_ref, first_ref, last_ref, firstp_ref, lastp_ref,
+                   packed, arrived, ids_out, ids_in, stats_out, stats_in,
+                   send_sem, recv_sem, isend_sem, irecv_sem, ssend_sem, srecv_sem):
     n_src, n_frame, n_tile = sizes
     devices = n_src * n_frame * n_tile
     rows, channels = feats_ref.shape
@@ -89,13 +91,41 @@
 
     lax.fori_loop(1, devices, greet, 0)
 
+    def row_copy(k):
+        at = pl.ds(pl.multiple_of(k * block, 16), block)
+        return pltpu.make_async_remote_copy(
+            src_ref=packed.at[at], dst_ref=arrived.at[at],
+            send_sem=send_sem.at[k], recv_sem=recv_sem.at[k],
+            device_id=coords(k), device_id_type=MESH,
+        )
+
+    def ids_copy(k):
+        return pltpu.make_async_remote_copy(
+            src_ref=ids_out.at[k], dst_ref=ids_in.at[k],
+            send_sem=isend_sem.at[k], recv_sem=irecv_sem.at[k],
+            device_id=coords(k), device_id_type=MESH,
+        )
+
+    def stats_copy(k):
+        return pltpu.make_async_remote_copy(
+            src_ref=stats_out, dst_ref=stats_in.at[k],
+            send_sem=ssend_sem.at[k], recv_sem=srecv_sem.at[k],
+            device_id=coords(k), device_id_type=MESH,
+        )
+
+    def each(lo, hi, act):
+        def body(k, carry):
+            act(k)
+            return carry
+
+        lax.fori_loop(lo, hi, body, 0)
+
     owner = info_ref[0:1, :]
     slot_hi = info_ref[1:2, :].astype(F32)
     slot_lo = info_ref[2:3, :].astype(F32)
     clip = info_ref[3:4, :]
 
-    owner_is = iota((devices, rows), 0) == owner
-    onehot = owner_is.astype(F32)
+    onehot = (iota((devices, rows), 0) == owner).astype(F32)
     onehot_b = onehot.astype(BF)
     span = 256
     before = (iota((span, span), 0) < iota((span, span), 1)).astype(F32).astype(BF)
@@ -108,42 +138,35 @@
         running = running + jnp.sum(part, axis=1, keepdims=True)
     rank = jnp.concatenate(ranks, axis=1).astype(jnp.int32)
     position = owner * block + rank
-    hi, mid, low = split3(feats_ref[...])
-    total = devices * block
-    chunk = total // 4
-    for start in range(0, total, chunk):
-        pick = (iota((chunk, rows), 0) + start == position).astype(F32).astype(BF)
-        packed[pl.ds(start, chunk), :] = encode(dot(pick, hi) + dot(pick, mid))
-
-    pl.semaphore_wait(barrier, devices - 1)
-
-    def row_copy(k):
-        return pltpu.make_async_remote_copy(
-            src_ref=packed.at[pl.ds(pl.multiple_of(k * block, 16), block)],
-            dst_ref=arrived_ref.at[pl.ds(pl.multiple_of(me * block, 16), block)],
-            send_sem=send_sem.at[k],
-            recv_sem=recv_sem.at[k],
-            device_id=coords(k),
-            device_id_type=MESH,
-        )
-
-    def send_rows(k, carry):
-        row_copy(k).start()
-        return carry
-
-    lax.fori_loop(1, devices, send_rows, 0)
-    arrived_ref[pl.ds(pl.multiple_of(me * block, 16), block), :] = packed[0:block, :]
 
     rank_is = (iota((128, rows), 0) == rank).astype(F32).astype(BF)
     contract = (((1,), (1,)), ((), ()))
     ids = 32.0 * lax.dot_general(
         (onehot * slot_hi).astype(BF), rank_is, contract, preferred_element_type=F32
     ) + lax.dot_general((onehot * slot_lo).astype(BF), rank_is, contract, preferred_element_type=F32)
+    ids_out[...] = ids[:, None, :]
+
+    feats = feats_ref[...]
+    hi = feats.astype(BF)
+    mid = (feats - hi.astype(F32)).astype(BF)
+    parts = 4
+    some = devices // parts
+    chunk = some * block
+    for p in range(parts):
+        pick = (iota((chunk, rows), 0) + p * chunk == position).astype(F32).astype(BF)
+        packed[pl.ds(p * chunk, chunk), :] = encode(dot(pick, hi) + dot(pick, mid))
+        if p == 0:
+            pl.semaphore_wait(barrier, devices - 1)
+            each(1, devices, lambda k: ids_copy(k).start())
+        each(max(1, p * some), (p + 1) * some, lambda k: row_copy(k).start())
+    arrived[0:block, :] = packed[0:block, :]
+    ids_in[0] = ids_out[0]
 
     in_clip = (iota((8, rows), 0) == clip).astype(F32)
     in_clip_b = in_clip.astype(BF)
     counts = jnp.sum(in_clip, axis=1, keepdims=True) * float(width)
-    sums = dot(in_clip_b, hi) + dot(in_clip_b, mid) + dot(in_clip_b, low)
+    s_hi, s_mid, s_low = split3(feats_ref[...])
+    sums = dot(in_clip_b, s_hi) + dot(in_clip_b, s_mid) + dot(in_clip_b, s_low)
     to_groups = group_matrix(channels, width)
     group_sums = dot_exact(sums, to_groups)
     own_lanes = clip_lanes()
@@ -159,86 +182,87 @@
     def lanes(x):
         return jnp.sum(jnp.where(own_lanes, x, 0.0), axis=0, keepdims=True)
 
-    line = iota((8, 128), 0)
+    line = iota((4, 128), 0)
     stats = jnp.where(
-        line == 1,
+        line == 0,
         lanes(group_sums),
-        jnp.where(line == 2, lanes(group_squares),
-                  jnp.where(line == 3, lanes(jnp.broadcast_to(counts, (8, 128))), 0.0)),
+        jnp.where(line == 1, lanes(group_squares), lanes(jnp.broadcast_to(counts, (8, 128)))),
     )
-    wide = (devices, 8, 128)
-    msg[...] = jnp.where(
-        iota(wide, 1) == 0,
-        jnp.broadcast_to(ids[:, None, :], wide),
-        jnp.broadcast_to(stats[None], wide),
-    )
-
-    def msg_copy(k):
-        return pltpu.make_async_remote_copy(
-            src_ref=msg.at[k],
-            dst_ref=msgs_ref.at[me],
-            send_sem=msend_sem.at[k],
-            recv_sem=mrecv_sem.at[k],
-            device_id=coords(k),
-            device_id_type=MESH,
-        )
-
-    def send_msg(k, carry):
-        msg_copy(k).start()
-        return carry
-
-    lax.fori_loop(1, devices, send_msg, 0)
-    msgs_ref[pl.ds(me, 1)] = msg[0:1]
-
-    def finish(k, carry):
-        row_copy(k).wait()
-        msg_copy(k).wait()
-        return carry
-
-    lax.fori_loop(1, devices, finish, 0)
-
-
-def place_kernel(clips_ref, targets_ref, msgs_ref, arrived_ref, gain_ref, bias_ref,
-                 features_ref, act_ref, first_ref, last_ref, firstp_ref, lastp_ref, mean_s, inv_s):
-    rows, channels = features_ref.shape
-    width = channels // GROUPS
-    sums = msgs_ref[:, 1, :]
-    squares = msgs_ref[:, 2, :]
-    counts = msgs_ref[:, 3, :]
+    stats_out[...] = stats
+    stats_in[0] = stats
+    each(1, devices, lambda k: stats_copy(k).start())
+
+    third = rows // 3
+    lane = iota((8, 128), 1)
+    for p in range(parts):
+        lo, end = p * some, (p + 1) * some
+        each(max(1, lo), end, lambda k: ids_copy(k).wait_recv())
+        pieces = []
+        for q in range(chunk // 128):
+            piece = jnp.zeros((8, 128), F32)
+            for j in range(some):
+                shift = j * block - q * 128
+                if shift + block <= 0 or shift >= 128:
+                    continue
+                line8 = jnp.broadcast_to(ids_in[lo + j], (8, 128))
+                if shift % 128:
+                    line8 = pltpu.roll(line8, shift % 128, 1)
+                piece = jnp.where((lane >= shift) & (lane < shift + block), line8, piece)
+            pieces.append(piece[0:1])
+        targets = jnp.concatenate(pieces, axis=1).astype(jnp.int32)
+        each(max(1, lo), end, lambda k: row_copy(k).wait_recv())
+        value = decode(arrived[pl.ds(p * chunk, chunk), :])
+        v_hi = value.astype(BF)
+        v_rest = (value - v_hi.astype(F32)).astype(BF)
+        for start in range(0, rows, third):
+            at = pl.ds(start, third)
+            pick = (iota((third, chunk), 0) + start == targets).astype(F32).astype(BF)
+            placed = dot(pick, v_hi) + dot(pick, v_rest)
+            if p == 0:
+                features_ref[at, :] = placed
+            else:
+                features_ref[at, :] += placed
+
+    each(1, devices, lambda k: stats_copy(k).wait_recv())
+    sums = stats_in[:, 0, :]
+    squares = stats_in[:, 1, :]
+    counts = stats_in[:, 2, :]
     total = jnp.sum(counts, axis=0, keepdims=True)
     mean = jnp.sum(sums, axis=0, keepdims=True) / total
     off = sums / jnp.maximum(counts, 1.0) - mean
     var = jnp.sum(squares + counts * (off * off), axis=0, keepdims=True) / total
     inv = 1.0 / jnp.sqrt(var + 1e-06)
     spread = group_matrix_t(channels, width)
-    own_lanes = clip_lanes()
-    mean_s[...] = dot_exact(jnp.where(own_lanes, mean, 0.0), spread)
-    inv_s[...] = dot_exact(jnp.where(own_lanes, inv, 0.0), spread)
+    clip_mean = dot_exact(jnp.where(own_lanes, mean, 0.0), spread)
+    clip_inv = dot_exact(jnp.where(own_lanes, inv, 0.0), spread)
     first_frame = lax.axis_index("frame") * FR_DEV
     plane = HR * WCOL
     first_ref[...] = jnp.zeros_like(first_ref)
     last_ref[...] = jnp.zeros_like(last_ref)
-    arrived = decode(arrived_ref[...])
-    hi = arrived.astype(BF)
-    rest = (arrived - hi.astype(F32)).astype(BF)
     for t in range(FR_DEV):
-        pick = (iota((plane, targets_ref.shape[1]), 0) + t * plane == targets_ref[...]).astype(F32).astype(BF)
-        x = dot(pick, hi) + dot(pick, rest)
-        features_ref[pl.ds(t * plane, plane), :] = x
-        c = clips_ref[first_frame + t]
-        normed = (x - mean_s[pl.ds(c, 1), :]) * inv_s[pl.ds(c, 1), :]
+        here = iota((8, channels), 0) == clips_ref[first_frame + t]
+        mean_t = jnp.sum(jnp.where(here, clip_mean, 0.0), axis=0, keepdims=True)
+        inv_t = jnp.sum(jnp.where(here, clip_inv, 0.0), axis=0, keepdims=True)
+        normed = (features_ref[pl.ds(t * plane, plane), :] - mean_t) * inv_t
         v = normed * gain_ref[...] + bias_ref[...]
         act = v / (1.0 + jnp.exp(-v))
         for h in range(HR):
-            slab = act[h * WCOL : (h + 1) * WCOL]
-            act_ref[t, h] = slab.astype(BF)
-            rounded = slab.astype(BF).astype(F32)
+            slab = act[h * WCOL : (h + 1) * WCOL].astype(BF)
+            act_ref[t, h] = slab
+            rounded = slab.astype(F32)
             first_ref[h, t : t + 1, :] = rounded[0:1]
             last_ref[h, t : t + 1, :] = rounded[WCOL - 1 : WCOL]
             if t >= FR_DEV - 2:
                 u = t - (FR_DEV - 2)
                 firstp_ref[u, h : h + 1, :] = rounded[0:1]
                 lastp_ref[u, h : h + 1, :] = rounded[WCOL - 1 : WCOL]
+
+    def sent(k):
+        row_copy(k).wait_send()
+        ids_copy(k).wait_send()
+        stats_copy(k).wait_send()
+
+    each(1, devices, sent)
 
 
 def decode_kernel(sizes, clips_ref, act_ref, first_ref, last_ref, firstp_ref, lastp_ref, features_ref, bias_ref,
@@ -418,32 +442,11 @@
     vmem = pl.BlockSpec(memory_space=pltpu.VMEM)
     smem = pl.BlockSpec(memory_space=pltpu.SMEM)
     dma = pltpu.SemaphoreType.DMA
-    arrived, msgs = pl.pallas_call(
-        functools.partial(reshard_kernel, sizes, block),
-        out_shape=(
-            jax.ShapeDtypeStruct((devices * block, channels), CODE),
-            jax.ShapeDtypeStruct((devices, 8, 128), F32),
-        ),
-        in_specs=[vmem] * 2,
-        out_specs=(vmem, vmem),
-        scratch_shapes=[
-            pltpu.VMEM((devices * block, channels), CODE),
-            pltpu.VMEM((devices, 8, 128), F32),
-            dma((devices,)),
-            dma((devices,)),
-            dma((devices,)),
-            dma((devices,)),
-        ],
-        compiler_params=pltpu.CompilerParams(
-            collective_id=0, has_side_effects=True, vmem_limit_bytes=VMEM_LIMIT
-        ),
-        name="reshard",
-    )(info, feats)
-    targets = msgs[:, 0, :block].reshape(1, devices * block).astype(jnp.int32)
     edge = jax.ShapeDtypeStruct((HR, 8, channels), F32)
     edge_p = jax.ShapeDtypeStruct((2, HR, channels), F32)
+    total = devices * block
     features, act, first, last, firstp, lastp = pl.pallas_call(
-        place_kernel,
+        functools.partial(reshard_kernel, sizes, block),
         out_shape=(
             jax.ShapeDtypeStruct((rows, channels), F32),
             jax.ShapeDtypeStruct((FR_DEV, HR, WCOL, channels), BF),
@@ -452,12 +455,21 @@
             edge_p,
             edge_p,
         ),
-        in_specs=[smem] + [vmem] * 5,
+        in_specs=[smem] + [vmem] * 4,
         out_specs=(vmem,) * 6,
-        scratch_shapes=[pltpu.VMEM((8, channels), F32)] * 2,
-        compiler_params=pltpu.CompilerParams(vmem_limit_bytes=VMEM_LIMIT),
-        name="place",
-    )(clip_ids, targets, msgs, arrived, norm_gain[None], norm_bias[None])
+        scratch_shapes=[
+            pltpu.VMEM((total, channels), CODE),
+            pltpu.VMEM((total, channels), CODE),
+            pltpu.VMEM((devices, 1, 128), F32),
+            pltpu.VMEM((devices, 1, 128), F32),
+            pltpu.VMEM((4, 128), F32),
+            pltpu.VMEM((devices, 4, 128), F32),
+        ] + [dma((devices,))] * 6,
+        compiler_params=pltpu.CompilerParams(
+            collective_id=0, has_side_effects=True, vmem_limit_bytes=VMEM_LIMIT
+        ),
+        name="reshard",
+    )(clip_ids, info, feats, norm_gain[None], norm_bias[None])
     return pl.pallas_call(
         functools.partial(decode_kernel, sizes),
         out_shape=jax.ShapeDtypeStruct((FR_DEV, HR, WCOL, channels), BF),

time: 102 us -> 90.5 us (0.89)
  Pallas kernels: 95 us -> 85.3 us
    pallas_call x1 -> x0, Pallas kernels: 11.2 us -> none  [shards(): pl.pallas_call(place_kernel, out_shape=(jax.ShapeDtypeStruct((rows, chann...]
    pallas_call x1, Pallas kernels: 30.8 us -> 32.2 us  [shards(): pl.pallas_call(functools.partial(decode_kernel, sizes), out_shape=jax.Sha...]
where the time goes in v3:
time: 90.5 us; the launch traced here: 90.3 us
  Pallas kernels  85.3 us (94%)
  local copies, waits for them, and re-layouts  2.75 us (3%)
  other arithmetic  2.12 us (2%)
    pallas_call x1, Pallas kernels, shards(): pl.pallas_call(functools.partial(reshard_kernel, sizes, block), out_shape...  53.2 us
    pallas_call x1, Pallas kernels, shards(): pl.pallas_call(functools.partial(decode_kernel, sizes), out_shape=jax.Sha...  32.2 us
    unnamed x1, local copies, waits for them, and re-layouts  2.73 us

profile of v3, /device:TPU:1, one launch (start us, length us, event | category | flops | bytes accessed | tf_op | source)
XLA Modules:
  0.0 90.3 jit_solution(588846929998287205)
XLA Ops:
  0.0 0.7 add_select_fusion.6
  0.8 0.7 select_reduce_fusion
  1.5 0.6 pad_add_fusion.info_ref
  2.2 53.2 %reshard.1 = (f32[1536,512]{1,0:T(8,128)}, bf16[6,8,32,512]{3,2,1,0:T(8,128)(2,1)}, f32[8,8,512]{2,1,0:T(8,128)}, f32[8,8,512]{2,1,0:T(8,128)}, f32[2,8,512]{2,1,0:T(8,128)}, /*index=5*/f32[2,8,512]{2,1,0:T(8,128)}) custom-call(s32[12]{0:T(128)} %clips_ref.3, s32[4,1536]{1,0:T(4,128)} %pad_add_fusion.info_ref, f32[1536,512]{1,0:T(8,128)} %feats_ref.1, ...), custom_call_target="tpu_custom_call" | custom-call | tf_op jit(solution)/shard_map/reshard/pallas_call | solution.py:448
  55.4 32.2 %halo_conv.1 = bf16[6,8,32,512]{3,2,1,0:T(8,128)(2,1)} custom-call(s32[12]{0:T(128)} %clips_ref.3, bf16[6,8,32,512]{3,2,1,0:T(8,128)(2,1)} %get-tuple-element.11.act_ref, f32[8,8,512]{2,1,0:T(8,128)} %get-tuple-element.12.first_ref, f32[8,8,512]{2,1,0:T(8,128)} %get-tuple-element.13.last_ref, f32[2,8,512]{2,1,0:T(8,128)} %get-tuple-element.14.firstp_ref, ...), custom_call_target="tpu_custom_call" | custom-call | tf_op jit(solution)/shard_map/halo_conv/pallas_call | solution.py:473
  87.5 2.7 %copy.9 = bf16[6,8,32,512]{3,2,1,0:T(8,128)(2,1)} copy(bf16[6,8,32,512]{3,2,1,0:T(8,128)(2,1)} %halo_conv.1) | data formatting | bytes 3145728
  (4 shorter events, 0.0 us)
